TPU v7x, 512 devices: a whole 4x8x8 slice. The times are simulated.
512 devices in a mesh: replica: 16 (over y, core), fsdp: 32 (over x, z).
Axes of the slice: x: 4, y: 8, z: 8, core: 2. Of those that a mesh axis runs over, the one named last changes fastest.
Arguments:
- momentum: float32 [16, 256, 14336], P('replica', 'fsdp'), may hold values from -6 to 6
- gradient: bfloat16 [16, 256, 14336], P('replica', 'fsdp'), may hold values from -6 to 6
- selection: int32 [16, 4, 224, 2], replicated, may hold values from 0 to 63, as said below
Outputs:
- residual_momentum: float32 [16, 256, 14336], P('replica', 'fsdp')
- update: float32 [256, 14336], P(None, 'fsdp')
Inputs may be any that keep to these rules, and one draw needn't show every extreme that they name: `selection`: for each replica and span, the 2 block numbers are distinct.
All inputs are finite; a program needn't handle non-finite values.
Results may differ from a plain program's by a relative error of at most 0.0003.
Values sent between devices are 32-bit elements; how exact they have to be, the bound alone decides.
A program may use at most 64 MiB of HBM per device.

v0:
```python
import jax
import jax.numpy as jnp
from jax import lax
from jax.sharding import PartitionSpec as P

SPAN_SIDE = 64
BLOCK_SIDE = 8
BLOCKS_KEPT = 2
decay_rate = 0.9
highest = lax.Precision.HIGHEST


def from_everyone(value, axis):
    size = lax.axis_size(axis)
    return lax.all_to_all(
        jnp.broadcast_to(value[None], (size, *value.shape)), axis, 0, 0, tiled=True
    )


def joined_along(tiles, dim):
    shape = list(tiles.shape[1:])
    shape[dim] *= tiles.shape[0]
    return jnp.moveaxis(tiles, 0, dim).reshape(shape)


def gathered_copies(value, axis, dim):
    tiles = from_everyone(value, axis)
    return joined_along(tiles, dim)


def cosine_table(side):
    freq = jnp.arange(side, dtype=jnp.float32)[:, None]
    place = jnp.arange(side, dtype=jnp.float32)[None, :]
    scale = jnp.where(freq == 0, jnp.sqrt(1.0 / side), jnp.sqrt(2.0 / side))
    return scale * jnp.cos(jnp.pi * (2.0 * place + 1.0) * freq / (2.0 * side))


def side_marks(index):
    per_side = SPAN_SIDE // BLOCK_SIDE
    return (index[..., None] == jnp.arange(per_side, dtype=jnp.int32)).astype(jnp.float32)


def pick_rows(index, tiles):
    return jnp.einsum("...p,pia->...ia", side_marks(index), tiles, precision=highest)


def local(momentum, gradient, selection):
    table = cosine_table(SPAN_SIDE)
    per_side = SPAN_SIDE // BLOCK_SIDE
    tiles = table.reshape(per_side, BLOCK_SIDE, SPAN_SIDE)
    zero = jnp.zeros((), jnp.int32)
    fsdp_count = lax.axis_size("fsdp")
    fsdp_rank = lax.axis_index("fsdp")
    replica_rank = lax.axis_index("replica")
    replicas = selection.shape[0]
    decayed = decay_rate * momentum[0] + gradient[0].astype(jnp.float32)
    rows_dev, width = decayed.shape
    rows_all = rows_dev * fsdp_count
    span_rows = rows_all // SPAN_SIDE
    local_cols = width // fsdp_count
    span_cols = local_cols // SPAN_SIDE
    all_cols = width // SPAN_SIDE
    group = SPAN_SIDE // rows_dev
    span_row_own = fsdp_rank // group
    square = BLOCK_SIDE * BLOCK_SIDE
    column_start = fsdp_rank * span_cols
    chosen_all = lax.dynamic_slice(
        selection, (zero, zero, column_start, zero), (replicas, span_rows, span_cols, BLOCKS_KEPT)
    )
    chosen_own = lax.dynamic_index_in_dim(chosen_all, replica_rank, 0, keepdims=False)
    row_own = pick_rows(chosen_own // per_side, tiles)
    col_own = pick_rows(chosen_own % per_side, tiles)
    mine_all = lax.dynamic_slice(
        selection, (replica_rank, span_row_own, zero, zero), (1, 1, all_cols, BLOCKS_KEPT)
    )
    mine_all = mine_all.reshape(all_cols, BLOCKS_KEPT)
    owned = lax.all_to_all(decayed, "fsdp", split_axis=1, concat_axis=0, tiled=True)
    spans = owned.reshape(span_rows, SPAN_SIDE, span_cols, SPAN_SIDE)
    kept = jnp.einsum("rckia,racb,rckjb->rckij", row_own, spans, col_own, precision=highest)
    kept = kept.reshape(span_rows, span_cols, BLOCKS_KEPT, square)
    packed = kept.reshape(1, span_rows, span_cols, BLOCKS_KEPT * square)
    piece = gathered_copies(packed, "replica", 0)
    count = piece.shape[0]
    values = piece.reshape(count, span_rows, span_cols, BLOCKS_KEPT, BLOCK_SIDE, BLOCK_SIDE)
    row_sel = pick_rows(chosen_all // per_side, tiles)
    col_sel = pick_rows(chosen_all % per_side, tiles)
    summed = jnp.einsum("qrckia,qrckij,qrckjb->racb", row_sel, values, col_sel, precision=highest)
    update = summed.reshape(rows_all, local_cols)
    own_values = kept.reshape(span_rows, span_cols, BLOCKS_KEPT, BLOCK_SIDE, BLOCK_SIDE)
    extracted = jnp.einsum(
        "rckia,rckij,rckjb->racb", row_own, own_values, col_own, precision=highest
    )
    extracted = extracted.reshape(rows_all, local_cols)
    taken = lax.all_to_all(extracted, "fsdp", split_axis=0, concat_axis=1, tiled=True)
    residual_momentum = decayed - taken
    return (residual_momentum[None], update)


def solution(mesh):
    placed = (P("replica", "fsdp", None), P("replica", "fsdp", None), P())
    return jax.shard_map(
        local,
        mesh=mesh,
        in_specs=placed,
        out_specs=(P("replica", "fsdp", None), P(None, "fsdp")),
        check_vma=False,
    )
```

profile of v0, /device:TPU:1, one launch (start us, length us, event | category | flops | bytes accessed | tf_op | source)
XLA Modules:
  0.0 84.9 jit_solution(9852488467808630540)
XLA Ops:
  0.6 0.0 copy-start.1
  0.6 1.2 %convert_add_fusion = f32[1,8,14336]{2,1,0:T(8,128)S(1)} fusion(bf16[1,8,14336]{2,1,0:T(8,128)(2,1)} %param.4, f32[1,8,14336]{2,1,0:T(8,128)} %param.3), kind=kLoop, calls=%fused_computation.9 | loop fusion | flops 344064 | bytes 1146880 | tf_op jit(solution)/shard_map/add | solution.py:56
  1.9 0.3 add.64
  2.1 1.1 %copy.44 = f32[8,32,448]{2,0,1:T(8,128)} copy(f32[8,32,448]{2,1,0:T(8,128)S(1)} %add.64) | data formatting | bytes 917504 | tf_op jit(solution)/shard_map/add | solution.py:56
  3.2 13.7 %all-to-all-start = ((f32[8,32,448]{2,0,1:T(8,128)}), f32[8,32,448]{2,0,1:T(8,128)S(1)}, u32[]{:S(2)}, u32[]{:S(2)}) async-start(f32[8,32,448]{2,0,1:T(8,128)} %copy.44), calls=%async_computation | async-start | bytes 1048576 | tf_op jit(solution)/shard_map/all_to_all | solution.py:77
  17.0 0.0 copy-done.1
  17.0 0.3 and_select_fusion.1
  17.3 0.1 constant_dynamic-slice_fusion
  17.4 0.1 copy.58
  17.6 0.1 copy.61
  17.7 0.4 fusion.30
  18.2 0.4 fusion.28
  18.6 3.6 %fusion.13 = f32[16,4,7,2,8,64]{5,0,4,3,2,1:T(8,128)} fusion(s32[16,4,7,2]{0,3,2,1:T(2,128)S(1)} %copy.58, f32[8,8]{0,1:T(8,128)S(1)} %multiply_add_fusion, f32[64]{0:T(128)S(1)} %add_multiply_fusion, f32[8,8]{0,1:T(8,128)S(1)} %compare_select_fusion), kind=kOutput, calls=%fused_computation.13 | convolution fusion | flops 44059648 | bytes 1839360 | tf_op jit(solution)/shard_map/...p,pia->...ia/dot_general | solution.py:44
  22.2 9.0 %all-to-all-done = f32[8,32,448]{2,0,1:T(8,128)S(1)} async-done(((f32[8,32,448]{2,0,1:T(8,128)}), f32[8,32,448]{2,0,1:T(8,128)S(1)}, u32[]{:S(2)}, u32[]{:S(2)}) %all-to-all-start) | async-done | bytes 458784 | tf_op jit(solution)/shard_map/all_to_all | solution.py:77
  31.3 0.2 reshape.116
  31.5 1.0 %fusion.10 = f32[4,7,64,2,8]{2,4,3,1,0:T(8,128)S(1)} fusion(f32[4,64,7,64,1]{3,2,1,0,4:T(8,128)S(1)} %bitcast.78, f32[4,7,2,8,64]{4,1,3,2,0:T(8,128)S(1)} %fusion.30), kind=kOutput, calls=%fused_computation.7 | convolution fusion | flops 22020096 | bytes 688128 | tf_op jit(solution)/shard_map/rckia,racb,rckjb->rckij/dot_general | solution.py:79
  32.5 0.5 fusion.19
  33.0 0.1 reshape.127
  33.2 0.7 broadcast_in_dim.15
  33.9 10.6 %all-to-all-start.2 = ((f32[16,1,4,7,128]{4,2,3,1,0:T(4,128)}), f32[16,1,4,7,128]{4,2,3,1,0:T(4,128)S(1)}, u32[]{:S(2)}, u32[]{:S(2)}) async-start(f32[16,1,4,7,128]{4,2,3,1,0:T(4,128)} %broadcast_in_dim.15), calls=%async_computation.2 | async-start | bytes 458752 | tf_op jit(solution)/shard_map/all_to_all | solution.py:15
  44.5 3.6 %fusion.16 = f32[16,4,7,2,8,64]{5,0,4,3,2,1:T(8,128)} fusion(s32[16,4,7,2]{0,3,2,1:T(2,128)S(1)} %copy.61, f32[8,8]{0,1:T(8,128)S(1)} %multiply_add_fusion, f32[64]{0:T(128)S(1)} %add_multiply_fusion, f32[8,8]{0,1:T(8,128)S(1)} %compare_select_fusion), kind=kOutput, calls=%fused_computation.15 | convolution fusion | flops 44059648 | bytes 1839360 | tf_op jit(solution)/shard_map/...p,pia->...ia/dot_general | solution.py:44
  48.1 0.6 fusion.21
  48.7 1.6 %convolution_bitcast_fusion = f32[4,64,7,64]{3,1,2,0:T(8,128)S(1)} fusion(f32[4,7,2,8,64]{4,3,2,1,0:T(8,128)S(1)} %fusion.21, f32[4,7,2,8,64]{4,1,3,2,0:T(8,128)S(1)} %fusion.28), kind=kOutput, calls=%fused_computation.5 | convolution fusion | flops 22020096 | bytes 688128 | tf_op jit(solution)/shard_map/rckia,rckij,rckjb->racb/dot_general | solution.py:90
  50.4 0.5 copy.54
  50.9 1.0 %all_to_all.29 = f32[32,8,448]{2,1,0:T(8,128)} reshape(f32[4,64,7,64]{3,2,1,0:T(8,128)S(1)} %copy.54) | data formatting | bytes 917504 | tf_op jit(solution)/shard_map/all_to_all | solution.py:94
  51.9 3.7 %all-to-all-done.2 = f32[16,1,4,7,128]{4,2,3,1,0:T(4,128)S(1)} async-done(((f32[16,1,4,7,128]{4,2,3,1,0:T(4,128)}), f32[16,1,4,7,128]{4,2,3,1,0:T(4,128)S(1)}, u32[]{:S(2)}, u32[]{:S(2)}) %all-to-all-start.2) | async-done | bytes 229408 | tf_op jit(solution)/shard_map/all_to_all | solution.py:15
  55.6 5.5 %all-to-all-start.1 = ((f32[32,8,448]{2,1,0:T(8,128)}), f32[32,8,448]{2,1,0:T(8,128)S(1)}, u32[]{:S(2)}, u32[]{:S(2)}) async-start(f32[32,8,448]{2,1,0:T(8,128)} %all_to_all.29), calls=%async_computation.1 | async-start | bytes 1048576 | tf_op jit(solution)/shard_map/all_to_all | solution.py:94
  61.1 0.5 copy.57
  61.7 4.1 %copy.73 = f32[16,4,7,2,8,8]{4,5,3,1,2,0:T(8,128)} copy(f32[16,4,7,2,8,8]{0,5,4,3,2,1:T(8,128)S(1)} %bitcast.77) | data formatting | bytes 458752 | tf_op jit(solution)/shard_map/reshape;reshape | solution.py:84
  65.7 0.0 copy-start
  65.7 9.2 %fusion.2 = f32[16,4,7,2,8,64]{5,4,3,1,2,0:T(8,128)S(1)} fusion(f32[16,4,7,2,8,8]{4,5,3,1,2,0:T(8,128)} %copy.73, f32[16,4,7,2,8,64]{5,0,4,3,2,1:T(8,128)} %fusion.13), kind=kOutput, calls=%fused_computation.2 | convolution fusion | flops 44040192 | bytes 3899392 | tf_op jit(solution)/shard_map/qrckia,qrckij,qrckjb->racb/dot_general | solution.py:87
  75.0 0.0 copy-done
  75.0 6.9 %fusion.5 = f32[4,64,7,64]{3,1,2,0:T(8,128)S(1)} fusion(f32[16,4,7,2,8,64]{5,0,4,3,2,1:T(8,128)S(1)} %copy-done, f32[16,4,7,2,8,64]{5,4,3,1,2,0:T(8,128)S(1)} %fusion.2), kind=kOutput, calls=%fused_computation.6 | convolution fusion | flops 352321536 | bytes 4128768 | tf_op jit(solution)/shard_map/qrckia,qrckij,qrckjb->racb/dot_general | solution.py:87
  81.9 0.4 copy.64
  82.2 1.3 %reshape.117 = f32[256,448]{0,1:T(8,128)} reshape(f32[4,64,7,64]{1,0,3,2:T(4,128)S(1)} %copy.64) | data formatting | bytes 917504 | tf_op jit(solution)/shard_map/reshape | solution.py:88
  83.6 0.0 all-to-all-done.1
  83.6 0.3 copy.55
  83.9 0.2 all_to_all.32
  84.1 0.8 sub.17
  (7 shorter events, 0.1 us)
Async XLA Ops:
  0.6 16.4 %copy-start.1 = (s32[16,4,224,2]{2,3,1,0:T(2,128)S(1)}, s32[16,4,224,2]{2,3,1,0:T(2,128)}, u32[]{:S(2)}) copy-start(s32[16,4,224,2]{2,3,1,0:T(2,128)} %param.5) | copy-start | bytes 344068
  3.2 28.0 %all-to-all-start = ((f32[8,32,448]{2,0,1:T(8,128)}), f32[8,32,448]{2,0,1:T(8,128)S(1)}, u32[]{:S(2)}, u32[]{:S(2)}) async-start(f32[8,32,448]{2,0,1:T(8,128)} %copy.44), calls=%async_computation | async-start | bytes 1048576 | tf_op jit(solution)/shard_map/all_to_all | solution.py:77
  33.9 21.7 %all-to-all-start.2 = ((f32[16,1,4,7,128]{4,2,3,1,0:T(4,128)}), f32[16,1,4,7,128]{4,2,3,1,0:T(4,128)S(1)}, u32[]{:S(2)}, u32[]{:S(2)}) async-start(f32[16,1,4,7,128]{4,2,3,1,0:T(4,128)} %broadcast_in_dim.15), calls=%async_computation.2 | async-start | bytes 458752 | tf_op jit(solution)/shard_map/all_to_all | solution.py:15
  55.6 28.0 %all-to-all-start.1 = ((f32[32,8,448]{2,1,0:T(8,128)}), f32[32,8,448]{2,1,0:T(8,128)S(1)}, u32[]{:S(2)}, u32[]{:S(2)}) async-start(f32[32,8,448]{2,1,0:T(8,128)} %all_to_all.29), calls=%async_computation.1 | async-start | bytes 1048576 | tf_op jit(solution)/shard_map/all_to_all | solution.py:94
  65.7 9.2 %copy-start = (f32[16,4,7,2,8,64]{5,0,4,3,2,1:T(8,128)S(1)}, f32[16,4,7,2,8,64]{5,0,4,3,2,1:T(8,128)}, u32[]{:S(2)}) copy-start(f32[16,4,7,2,8,64]{5,0,4,3,2,1:T(8,128)} %fusion.16) | copy-start | bytes 5505028
where the time goes:
time: 85.4 us; the launch traced here: 84.9 us
  starting transfers between devices  29.9 us (35%)
  matrix products  27.9 us (33%)
  waiting for transfers between devices  12.7 us (15%)
  local copies, waits for them, and re-layouts  11.2 us (13%)
  other arithmetic  2.38 us (3%)
    dot_general x2, matrix products, local(): jnp.einsum('qrckia,qrckij,qrckjb->racb', row_sel, values, col_sel, precis...  16.1 us
    all_to_all x1, starting transfers between devices, local(): lax.all_to_all(decayed, 'fsdp', split_axis=1, concat_axis=0, tiled=True)  13.7 us
    all_to_all x1, starting transfers between devices, from_everyone(): lax.all_to_all(jnp.broadcast_to(value[None], (size, *value.shape)), axis,...  10.6 us
    all_to_all x1, waiting for transfers between devices, local(): lax.all_to_all(decayed, 'fsdp', split_axis=1, concat_axis=0, tiled=True)  9.05 us
    dot_general x4, matrix products, pick_rows(): jnp.einsum('...p,pia->...ia', side_marks(index), tiles, precision=highest)  8.08 us
    all_to_all x1, starting transfers between devices, local(): lax.all_to_all(extracted, 'fsdp', split_axis=0, concat_axis=1, tiled=True)  5.52 us
    another operation x1, local copies, waits for them, and re-layouts, local(): piece.reshape(count, span_rows, span_cols, BLOCKS_KEPT, BLOCK_SIDE, BLOCK...  4.08 us
    all_to_all x1, waiting for transfers between devices, from_everyone(): lax.all_to_all(jnp.broadcast_to(value[None], (size, *value.shape)), axis,...  3.65 us
  transfers between devices with their start and end apart: 3, of which 2 were waited for; matrix products, arithmetic and copies ran while one was open for 40% of the time, Pallas kernels for 0%

commit v1 on v0

--- a/solution.py
+++ b/solution.py
@@ -91,7 +91,12 @@
         "rckia,rckij,rckjb->racb", row_own, own_values, col_own, precision=highest
     )
     extracted = extracted.reshape(rows_all, local_cols)
-    taken = lax.all_to_all(extracted, "fsdp", split_axis=0, concat_axis=1, tiled=True)
+    taken = jnp.concatenate(
+        lax.all_to_all(
+            jnp.stack(jnp.split(extracted, lax.psum(1, "fsdp"), 0), axis=0), "fsdp", 0, 0
+        ),
+        1,
+    )
     residual_momentum = decayed - taken
     return (residual_momentum[None], update)
 

time: 85.4 us -> 132 us (1.55)
  local copies, waits for them, and re-layouts: 11.2 us -> 64.2 us
  waiting for transfers between devices: 12.7 us -> 5.45 us
    another operation x0 -> x35, local copies, waits for them, and re-layouts: none -> 33.8 us  [local(): jnp.stack(jnp.split(extracted, lax.psum(1, 'fsdp'), 0), axis=0)]
    unnamed x4 -> x65, local copies, waits for them, and re-layouts: 0.01 us -> 18.7 us
    all_to_all x1, waiting for transfers between devices: 3.65 us -> 0.01 us  [from_everyone(): lax.all_to_all(jnp.broadcast_to(value[None], (size, *value.shape)), axis,...]
    all_to_all x1, waiting for transfers between devices: 9.05 us -> 5.44 us  [local(): lax.all_to_all(decayed, 'fsdp', split_axis=1, concat_axis=0, tiled=True)]
    all_to_all x3 -> x0, local copies, waits for them, and re-layouts: 1.55 us -> none  [local(): lax.all_to_all(extracted, 'fsdp', split_axis=0, concat_axis=1, tiled=True)]
  transfers between devices with their start and end apart: 3 -> 3, of which waited for: 2 -> 1; matrix products, arithmetic and copies ran while one was open for 40% -> 38% of each run, Pallas kernels for 0% -> 0%
where the time goes in v1:
time: 132 us; the launch traced here: 131 us
  local copies, waits for them, and re-layouts  64.2 us (49%)
  starting transfers between devices  29.7 us (22%)
  matrix products  28.2 us (21%)
  waiting for transfers between devices  5.45 us (4%)
  other arithmetic  2.38 us (2%)
    another operation x35, local copies, waits for them, and re-layouts, local(): jnp.stack(jnp.split(extracted, lax.psum(1, 'fsdp'), 0), axis=0)  33.8 us
    unnamed x65, local copies, waits for them, and re-layouts  18.7 us
    dot_general x2, matrix products, local(): jnp.einsum('qrckia,qrckij,qrckjb->racb', row_sel, values, col_sel, precis...  16.3 us
    all_to_all x1, starting transfers between devices, local(): lax.all_to_all(decayed, 'fsdp', split_axis=1, concat_axis=0, tiled=True)  13.7 us
    all_to_all x1, starting transfers between devices, from_everyone(): lax.all_to_all(jnp.broadcast_to(value[None], (size, *value.shape)), axis,...  10.6 us
    dot_general x4, matrix products, pick_rows(): jnp.einsum('...p,pia->...ia', side_marks(index), tiles, precision=highest)  8.09 us
    all_to_all x1, waiting for transfers between devices, local(): lax.all_to_all(decayed, 'fsdp', split_axis=1, concat_axis=0, tiled=True)  5.44 us
    all_to_all x1, starting transfers between devices, local(): lax.all_to_all(jnp.stack(jnp.split(extracted, lax.psum(1, 'fsdp'), 0), ax...  5.36 us
  transfers between devices with their start and end apart: 3, of which 1 were waited for; matrix products, arithmetic and copies ran while one was open for 38% of the time, Pallas kernels for 0%

profile of v1, /device:TPU:1, one launch (start us, length us, event | category | flops | bytes accessed | tf_op | source)
XLA Modules:
  0.0 130.9 jit_solution(15431540403540028077)
XLA Ops:
  0.6 1.2 convert_add_fusion
  2.1 1.1 copy.107
  3.2 13.7 %all-to-all-start = ((f32[8,32,448]{2,0,1:T(8,128)}), f32[8,32,448]{2,0,1:T(8,128)S(1)}, u32[]{:S(2)}, u32[]{:S(2)}) async-start(f32[8,32,448]{2,0,1:T(8,128)} %copy.107), calls=%async_computation | async-start | bytes 1048576 | tf_op jit(solution)/shard_map/all_to_all | solution.py:77
  18.6 3.6 %fusion.13 = f32[16,4,7,2,8,64]{5,0,4,3,2,1:T(8,128)} fusion(s32[16,4,7,2]{0,3,2,1:T(2,128)S(1)} %copy.153, f32[8,8]{0,1:T(8,128)S(1)} %multiply_add_fusion, f32[64]{0:T(128)S(1)} %add_multiply_fusion, f32[8,8]{0,1:T(8,128)S(1)} %compare_select_fusion), kind=kOutput, calls=%fused_computation.45 | convolution fusion | flops 44059648 | bytes 1839360 | tf_op jit(solution)/shard_map/...p,pia->...ia/dot_general | solution.py:44
  22.2 3.6 %fusion.16 = f32[16,4,7,2,8,64]{5,0,4,3,2,1:T(8,128)} fusion(s32[16,4,7,2]{0,3,2,1:T(2,128)S(1)} %copy.156, f32[8,8]{0,1:T(8,128)S(1)} %multiply_add_fusion, f32[64]{0:T(128)S(1)} %add_multiply_fusion, f32[8,8]{0,1:T(8,128)S(1)} %compare_select_fusion), kind=kOutput, calls=%fused_computation.47 | convolution fusion | flops 44059648 | bytes 1839360 | tf_op jit(solution)/shard_map/...p,pia->...ia/dot_general | solution.py:44
  25.8 5.4 %all-to-all-done = f32[8,32,448]{2,0,1:T(8,128)S(1)} async-done(((f32[8,32,448]{2,0,1:T(8,128)}), f32[8,32,448]{2,0,1:T(8,128)S(1)}, u32[]{:S(2)}, u32[]{:S(2)}) %all-to-all-start) | async-done | bytes 458784 | tf_op jit(solution)/shard_map/all_to_all | solution.py:77
  31.5 1.0 fusion.10
  33.0 0.6 fusion.21
  33.7 1.6 %convolution_bitcast_fusion = f32[4,64,7,64]{3,1,2,0:T(8,128)S(1)} fusion(f32[4,7,2,8,64]{4,3,2,1,0:T(8,128)S(1)} %fusion.21, f32[4,7,2,8,64]{4,1,3,2,0:T(8,128)S(1)} %fusion.28), kind=kOutput, calls=%fused_computation.5 | convolution fusion | flops 22020096 | bytes 688128 | tf_op jit(solution)/shard_map/rckia,rckij,rckjb->racb/dot_general | solution.py:90
  36.2 2.3 %slice_bitcast_fusion.19 = (f32[1,8,448]{1,2,0:T(8,128)}, f32[1,8,448]{1,2,0:T(8,128)}, f32[1,8,448]{1,2,0:T(8,128)}, f32[1,8,448]{1,2,0:T(8,128)}, f32[1,8,448]...) fusion(f32[256,448]{0,1:T(8,128)S(1)} %reshape.121), kind=kLoop, calls=%fused_computation.29 | loop fusion | bytes 372736 | tf_op jit(solution)/shard_map/stack | solution.py:96
  38.6 2.4 %slice_bitcast_fusion = (f32[1,8,448]{1,2,0:T(8,128)S(1)}, f32[1,8,448]{1,2,0:T(8,128)S(1)}, f32[1,8,448]{1,2,0:T(8,128)S(1)}, f32[1,8,448]{1,2,0:T(8,128)S(1)},...) fusion(f32[256,448]{0,1:T(8,128)S(1)} %reshape.121), kind=kLoop, calls=%fused_computation.10 | loop fusion | bytes 544768 | tf_op jit(solution)/shard_map/stack | solution.py:96
  41.0 0.7 reshape.134
  41.7 1.1 copy.118
  42.8 0.6 constant_dynamic-update-slice_fusion.31
  43.4 1.6 %copy.119 = f32[1,8,448]{2,1,0:T(8,128)} copy(f32[1,8,448]{1,2,0:T(8,128)} %get-tuple-element.32) | data formatting | bytes 28672 | tf_op jit(solution)/shard_map/stack | solution.py:96
  45.0 1.6 %copy.120 = f32[1,8,448]{2,1,0:T(8,128)} copy(f32[1,8,448]{1,2,0:T(8,128)} %get-tuple-element.31) | data formatting | bytes 28672 | tf_op jit(solution)/shard_map/stack | solution.py:96
  46.7 1.6 %copy.121 = f32[1,8,448]{2,1,0:T(8,128)} copy(f32[1,8,448]{1,2,0:T(8,128)} %get-tuple-element.30) | data formatting | bytes 28672 | tf_op jit(solution)/shard_map/stack | solution.py:96
  48.3 1.6 %copy.122 = f32[1,8,448]{2,1,0:T(8,128)} copy(f32[1,8,448]{1,2,0:T(8,128)} %get-tuple-element.29) | data formatting | bytes 28672 | tf_op jit(solution)/shard_map/stack | solution.py:96
  49.9 1.6 %copy.123 = f32[1,8,448]{2,1,0:T(8,128)} copy(f32[1,8,448]{1,2,0:T(8,128)} %get-tuple-element.28) | data formatting | bytes 28672 | tf_op jit(solution)/shard_map/stack | solution.py:96
  51.6 1.6 %copy.124 = f32[1,8,448]{2,1,0:T(8,128)} copy(f32[1,8,448]{1,2,0:T(8,128)} %get-tuple-element.27) | data formatting | bytes 28672 | tf_op jit(solution)/shard_map/stack | solution.py:96
  53.2 1.6 %copy.125 = f32[1,8,448]{2,1,0:T(8,128)} copy(f32[1,8,448]{1,2,0:T(8,128)} %get-tuple-element.26) | data formatting | bytes 28672 | tf_op jit(solution)/shard_map/stack | solution.py:96
  54.8 1.6 %copy.126 = f32[1,8,448]{2,1,0:T(8,128)} copy(f32[1,8,448]{1,2,0:T(8,128)} %get-tuple-element.25) | data formatting | bytes 28672 | tf_op jit(solution)/shard_map/stack | solution.py:96
  56.5 1.6 %copy.127 = f32[1,8,448]{2,1,0:T(8,128)} copy(f32[1,8,448]{1,2,0:T(8,128)} %get-tuple-element.24) | data formatting | bytes 28672 | tf_op jit(solution)/shard_map/stack | solution.py:96
  58.1 1.6 %copy.128 = f32[1,8,448]{2,1,0:T(8,128)} copy(f32[1,8,448]{1,2,0:T(8,128)} %get-tuple-element.23) | data formatting | bytes 28672 | tf_op jit(solution)/shard_map/stack | solution.py:96
  59.7 1.6 %copy.129 = f32[1,8,448]{2,1,0:T(8,128)} copy(f32[1,8,448]{1,2,0:T(8,128)} %get-tuple-element.22) | data formatting | bytes 28672 | tf_op jit(solution)/shard_map/stack | solution.py:96
  61.4 1.6 %copy.130 = f32[1,8,448]{2,1,0:T(8,128)} copy(f32[1,8,448]{1,2,0:T(8,128)} %get-tuple-element.21) | data formatting | bytes 28672 | tf_op jit(solution)/shard_map/stack | solution.py:96
  63.0 1.0 copy.131
  64.1 1.0 copy.132
  65.1 1.0 copy.133
  66.2 1.0 copy.134
  67.2 1.0 copy.135
  68.2 1.0 copy.136
  70.9 0.7 copy.178
  71.6 0.7 broadcast_in_dim.15
  72.4 10.6 %all-to-all-start.2 = ((f32[16,1,4,7,128]{4,2,3,1,0:T(4,128)}), f32[16,1,4,7,128]{4,2,3,1,0:T(4,128)S(1)}, u32[]{:S(2)}, u32[]{:S(2)}) async-start(f32[16,1,4,7,128]{4,2,3,1,0:T(4,128)} %broadcast_in_dim.15), calls=%async_computation.2 | async-start | bytes 458752 | tf_op jit(solution)/shard_map/all_to_all | solution.py:15
  83.0 0.6 constant_dynamic-update-slice_fusion.30
  85.4 0.6 constant_dynamic-update-slice_fusion.26
  89.0 0.6 constant_dynamic-update-slice_fusion.20
  89.6 0.6 constant_dynamic-update-slice_fusion.19
  95.0 0.6 constant_dynamic-update-slice_fusion.10
  99.2 0.6 constant_dynamic-update-slice_fusion.3
  101.0 0.6 constant_dynamic-update-slice_fusion
  101.6 5.4 %all-to-all-start.1 = ((f32[32,8,448]{2,1,0:T(8,128)}), f32[32,8,448]{2,1,0:T(8,128)S(1)}, u32[]{:S(2)}, u32[]{:S(2)}) async-start(f32[32,8,448]{2,1,0:T(8,128)} %constant_dynamic-update-slice_fusion), calls=%async_computation.1 | async-start | bytes 1048576 | tf_op jit(solution)/shard_map/all_to_all | solution.py:95
  107.5 4.0 %copy.168 = f32[16,4,7,2,8,8]{4,5,3,1,2,0:T(8,128)} copy(f32[16,4,7,2,8,8]{0,5,4,3,2,1:T(8,128)S(1)} %bitcast.143) | data formatting | bytes 458752 | tf_op jit(solution)/shard_map/reshape;reshape | solution.py:84
  111.5 9.4 %fusion.2 = f32[16,4,7,2,8,64]{5,4,3,1,2,0:T(8,128)S(1)} fusion(f32[16,4,7,2,8,8]{4,5,3,1,2,0:T(8,128)} %copy.168, f32[16,4,7,2,8,64]{5,0,4,3,2,1:T(8,128)} %fusion.13), kind=kOutput, calls=%fused_computation.2 | convolution fusion | flops 44040192 | bytes 3899392 | tf_op jit(solution)/shard_map/qrckia,qrckij,qrckjb->racb/dot_general | solution.py:87
  121.0 6.9 %fusion.5 = f32[4,64,7,64]{3,1,2,0:T(8,128)S(1)} fusion(f32[16,4,7,2,8,64]{5,0,4,3,2,1:T(8,128)S(1)} %copy-done, f32[16,4,7,2,8,64]{5,4,3,1,2,0:T(8,128)S(1)} %fusion.2), kind=kOutput, calls=%fused_computation.6 | convolution fusion | flops 352321536 | bytes 4128768 | tf_op jit(solution)/shard_map/qrckia,qrckij,qrckjb->racb/dot_general | solution.py:87
  128.2 1.3 %reshape.124 = f32[256,448]{0,1:T(8,128)} reshape(f32[4,64,7,64]{1,0,3,2:T(4,128)S(1)} %copy.159) | data formatting | bytes 917504 | tf_op jit(solution)/shard_map/reshape | solution.py:88
  130.1 0.8 sub.17
  (94 shorter events, 20.9 us)
Async XLA Ops:
  0.6 16.4 %copy-start.16 = (s32[16,4,224,2]{2,3,1,0:T(2,128)S(1)}, s32[16,4,224,2]{2,3,1,0:T(2,128)}, u32[]{:S(2)}) copy-start(s32[16,4,224,2]{2,3,1,0:T(2,128)} %param.5) | copy-start | bytes 344068
  3.2 28.0 %all-to-all-start = ((f32[8,32,448]{2,0,1:T(8,128)}), f32[8,32,448]{2,0,1:T(8,128)S(1)}, u32[]{:S(2)}, u32[]{:S(2)}) async-start(f32[8,32,448]{2,0,1:T(8,128)} %copy.107), calls=%async_computation | async-start | bytes 1048576 | tf_op jit(solution)/shard_map/all_to_all | solution.py:77
  40.9 28.5 %copy-start.2 = (f32[1,8,448]{1,2,0:T(8,128)S(1)}, f32[1,8,448]{1,2,0:T(8,128)}, u32[]{:S(2)}) copy-start(f32[1,8,448]{1,2,0:T(8,128)} %get-tuple-element.13) | copy-start | bytes 43012
  41.0 28.6 %copy-start.1 = (f32[1,8,448]{1,2,0:T(8,128)S(1)}, f32[1,8,448]{1,2,0:T(8,128)}, u32[]{:S(2)}) copy-start(f32[1,8,448]{1,2,0:T(8,128)} %get-tuple-element.12) | copy-start | bytes 43012
  41.7 27.6 %copy-start.3 = (f32[1,8,448]{1,2,0:T(8,128)S(1)}, f32[1,8,448]{1,2,0:T(8,128)}, u32[]{:S(2)}) copy-start(f32[1,8,448]{1,2,0:T(8,128)} %get-tuple-element.14) | copy-start | bytes 43012
  69.4 13.6 %copy-start.14 = (f32[1,8,448]{2,1,0:T(8,128)S(1)}, f32[1,8,448]{2,1,0:T(8,128)}, u32[]{:S(2)}) copy-start(f32[1,8,448]{2,1,0:T(8,128)} %copy.119) | copy-start | bytes 43012
  69.4 14.2 %copy-start.15 = (f32[1,8,448]{2,1,0:T(8,128)S(1)}, f32[1,8,448]{2,1,0:T(8,128)}, u32[]{:S(2)}) copy-start(f32[1,8,448]{2,1,0:T(8,128)} %copy.120) | copy-start | bytes 43012
  69.4 14.8 %copy-start.13 = (f32[1,8,448]{2,1,0:T(8,128)S(1)}, f32[1,8,448]{2,1,0:T(8,128)}, u32[]{:S(2)}) copy-start(f32[1,8,448]{2,1,0:T(8,128)} %copy.121) | copy-start | bytes 43012
  69.4 15.4 %copy-start.12 = (f32[1,8,448]{2,1,0:T(8,128)S(1)}, f32[1,8,448]{2,1,0:T(8,128)}, u32[]{:S(2)}) copy-start(f32[1,8,448]{2,1,0:T(8,128)} %copy.122) | copy-start | bytes 43012
  69.4 16.0 %copy-start.11 = (f32[1,8,448]{2,1,0:T(8,128)S(1)}, f32[1,8,448]{2,1,0:T(8,128)}, u32[]{:S(2)}) copy-start(f32[1,8,448]{2,1,0:T(8,128)} %copy.123) | copy-start | bytes 43012
  69.4 16.6 %copy-start.10 = (f32[1,8,448]{2,1,0:T(8,128)S(1)}, f32[1,8,448]{2,1,0:T(8,128)}, u32[]{:S(2)}) copy-start(f32[1,8,448]{2,1,0:T(8,128)} %copy.124) | copy-start | bytes 43012
  69.4 17.2 %copy-start.9 = (f32[1,8,448]{2,1,0:T(8,128)S(1)}, f32[1,8,448]{2,1,0:T(8,128)}, u32[]{:S(2)}) copy-start(f32[1,8,448]{2,1,0:T(8,128)} %copy.125) | copy-start | bytes 43012
  69.4 17.8 %copy-start.8 = (f32[1,8,448]{2,1,0:T(8,128)S(1)}, f32[1,8,448]{2,1,0:T(8,128)}, u32[]{:S(2)}) copy-start(f32[1,8,448]{2,1,0:T(8,128)} %copy.126) | copy-start | bytes 43012
  69.4 18.4 %copy-start.7 = (f32[1,8,448]{2,1,0:T(8,128)S(1)}, f32[1,8,448]{2,1,0:T(8,128)}, u32[]{:S(2)}) copy-start(f32[1,8,448]{2,1,0:T(8,128)} %copy.127) | copy-start | bytes 43012
  69.5 18.9 %copy-start.6 = (f32[1,8,448]{2,1,0:T(8,128)S(1)}, f32[1,8,448]{2,1,0:T(8,128)}, u32[]{:S(2)}) copy-start(f32[1,8,448]{2,1,0:T(8,128)} %copy.128) | copy-start | bytes 43012
  69.5 19.5 %copy-start.4 = (f32[1,8,448]{2,1,0:T(8,128)S(1)}, f32[1,8,448]{2,1,0:T(8,128)}, u32[]{:S(2)}) copy-start(f32[1,8,448]{2,1,0:T(8,128)} %copy.129) | copy-start | bytes 43012
  69.5 20.1 %copy-start.5 = (f32[1,8,448]{2,1,0:T(8,128)S(1)}, f32[1,8,448]{2,1,0:T(8,128)}, u32[]{:S(2)}) copy-start(f32[1,8,448]{2,1,0:T(8,128)} %copy.130) | copy-start | bytes 43012
  72.4 29.2 %all-to-all-start.2 = ((f32[16,1,4,7,128]{4,2,3,1,0:T(4,128)}), f32[16,1,4,7,128]{4,2,3,1,0:T(4,128)S(1)}, u32[]{:S(2)}, u32[]{:S(2)}) async-start(f32[16,1,4,7,128]{4,2,3,1,0:T(4,128)} %broadcast_in_dim.15), calls=%async_computation.2 | async-start | bytes 458752 | tf_op jit(solution)/shard_map/all_to_all | solution.py:15
  101.6 27.9 %all-to-all-start.1 = ((f32[32,8,448]{2,1,0:T(8,128)}), f32[32,8,448]{2,1,0:T(8,128)S(1)}, u32[]{:S(2)}, u32[]{:S(2)}) async-start(f32[32,8,448]{2,1,0:T(8,128)} %constant_dynamic-update-slice_fusion), calls=%async_computation.1 | async-start | bytes 1048576 | tf_op jit(solution)/shard_map/all_to_all | solution.py:95
  111.5 9.4 %copy-start = (f32[16,4,7,2,8,64]{5,0,4,3,2,1:T(8,128)S(1)}, f32[16,4,7,2,8,64]{5,0,4,3,2,1:T(8,128)}, u32[]{:S(2)}) copy-start(f32[16,4,7,2,8,64]{5,0,4,3,2,1:T(8,128)} %fusion.16) | copy-start | bytes 5505028
